TPU v7x, 128 devices: a whole 4x4x4 slice. The times are simulated.
128 devices in a mesh: kr: 8 (over x, z_lo), kc: 16 (over z_hi, y, core).
Axes of the slice: x: 4, y: 4, z: 4 (z_hi: 2, z_lo: 2; z = z_hi * 2 + z_lo), core: 2. Of those that a mesh axis runs over, the one named last changes fastest.
Arguments:
- densities: bfloat16 [128, 64, 2048], P('kc', None, 'kr'), may hold values from -0.890625 to 0.890625
- screened: bfloat16 [16, 2048, 2048], P(None, 'kr', 'kc'), may hold values from -1 to 3, as said below
- q_table: int32 [128, 128], replicated, may hold values from 0 to 15, as said below
Outputs:
- kernel: float32 [8192, 8192], P('kr', 'kc')
Inputs may be any that keep to these rules, and one draw needn't show every extreme that they name: screened is symmetric in its last two dimensions. q_table[k, k'] = (pos[k] - pos[k']) mod 16 for integer grid positions pos of the k points.
All inputs are finite; a program needn't handle non-finite values.
Results may differ from a plain program's by a relative error of at most 0.0025.
Values may be sent and summed in bfloat16 or wider, within the bound.
A program may use at most 128 MiB of HBM per device.

v0:
```python
import jax
import jax.numpy as jnp
from jax import lax
from jax.sharding import PartitionSpec as P


def local(densities, screened, q_table):
    block_len, pair_count, g_slice = densities.shape
    q_count = screened.shape[0]
    column = lax.all_gather(densities, "kr", axis=2, tiled=True)
    col_matrix = column.reshape(block_len * pair_count, column.shape[2])
    w_whole = lax.all_gather(screened, "kc", axis=2, tiled=True)
    y_sum = jnp.einsum("qgh,mh->qmg", w_whole, col_matrix, preferred_element_type=jnp.float32)
    screen_cols = y_sum.astype(jnp.bfloat16).reshape(q_count, block_len, pair_count, g_slice)
    row_dens = lax.all_gather(densities, "kc", axis=0, tiled=True)
    k_total = row_dens.shape[0]
    col_index = lax.axis_index("kc")
    q_columns = lax.dynamic_slice_in_dim(q_table, col_index * block_len, block_len, 1)
    picker = jnp.arange(block_len)[None, :]

    def block_product(row_block):
        row_slice = lax.dynamic_slice_in_dim(row_dens, row_block * block_len, block_len, 0)
        q_block = lax.dynamic_slice_in_dim(q_columns, row_block * block_len, block_len, 0)
        chosen = screen_cols[q_block, picker]
        return jnp.einsum("kpg,kjrg->kpjr", row_slice, chosen, preferred_element_type=jnp.float32)

    def one_block(row_block, kernel_slab):
        partial_value = block_product(row_block)
        return lax.dynamic_update_slice_in_dim(kernel_slab, partial_value, row_block * block_len, 0)

    slab_start = jnp.zeros((k_total, pair_count, block_len, pair_count), jnp.float32)
    kernel_slab = lax.fori_loop(0, col_index + 1, one_block, slab_start)
    flat = kernel_slab.reshape(k_total * pair_count, block_len * pair_count)
    return lax.psum_scatter(flat, "kr", scatter_dimension=0, tiled=True)


def solution(mesh):
    return jax.shard_map(
        local,
        mesh=mesh,
        in_specs=(P("kc", None, "kr"), P(None, "kr", "kc"), P()),
        out_specs=P("kr", "kc"),
        check_vma=False,
    )
```

profile of v0, /device:TPU:81, one launch (start us, length us, event | category | flops | bytes accessed | tf_op | source)
XLA Modules:
  0.0 744.3 jit_solution(14234385847299710210)
XLA Ops:
  8.9 59.1 %all-gather.6.cloned.1.call-done = bf16[8,64,2048]{2,1,0:T(8,128)(2,1)} async-done(((bf16[8,64,256]{2,1,0:T(8,128)(2,1)}), bf16[8,64,2048]{2,1,0:T(8,128)(2,1)}) %all-gather.6.cloned.1.call-update) | async-done | bytes 2097168 | tf_op jit(solution)/shard_map/all_gather | solution.py:10
  68.0 123.4 %all-gather.8.cloned.1.call-done = bf16[16,256,2048]{2,1,0:T(8,128)(2,1)} async-done(((bf16[16,256,128]{2,1,0:T(8,128)(2,1)}), bf16[16,256,2048]{2,1,0:T(8,128)(2,1)}) %all-gather.8.cloned.1.call-update) | async-done | bytes 16777232 | tf_op jit(solution)/shard_map/all_gather | solution.py:12
  191.4 14.4 %convolution_convert_fusion = bf16[512,16,256]{2,0,1:T(8,128)(2,1)} fusion(bf16[512,2048,1]{1,0,2:T(8,128)(2,1)} %bitcast.33, bf16[16,256,2048]{2,1,0:T(8,128)(2,1)} %all-gather.8.cloned.1.call-done), kind=kOutput, calls=%fused_computation.14 | convolution fusion | flops 8592031744 | bytes 23068672 | tf_op jit(solution)/shard_map/qgh,mh->qmg/dot_general | solution.py:13
  205.8 42.8 %all-gather.4.cloned.1.call-done = bf16[128,64,256]{2,1,0:T(8,128)(2,1)} async-done(((bf16[8,64,256]{2,1,0:T(8,128)(2,1)}), bf16[128,64,256]{2,1,0:T(8,128)(2,1)}) %all-gather.4.cloned.1.call-update) | async-done | bytes 4194320 | tf_op jit(solution)/shard_map/all_gather | solution.py:15
  248.6 11.1 %broadcast_in_dim.12.clone = f32[128,64,8,64]{3,2,1,0:T(8,128)} broadcast(f32[]{:T(128)} %constant.3.clone.1), dimensions={} | broadcast | bytes 16777220 | tf_op jit(solution)/shard_map/broadcast_in_dim | solution.py:31
  259.7 106.4 %while.11 = (s32[]{:T(128)}, f32[128,64,8,64]{3,2,1,0:T(8,128)}, s32[]{:T(128)}, bf16[128,64,256]{2,1,0:T(8,128)(2,1)}, s32[128,8]{1,0:T(8,128)S(1)}, /*index=5*...) while((s32[]{:T(128)}, f32[128,64,8,64]{3,2,1,0:T(8,128)}, ...), condition=%wide.region_1.0_spmd.clone, body=%wide.region_0.0_spmd.clone.sunk | while | flops 134218128 | bytes 10749663 | solution.py:32
  259.8 2.9 gather_fusion
  262.7 2.1 fusion.23
  264.8 2.5 copy_dynamic-update-slice_fusion.2
  267.4 2.9 gather_fusion
  270.3 2.1 fusion.23
  272.4 2.5 copy_dynamic-update-slice_fusion.2
  275.0 2.9 gather_fusion
  277.9 2.1 fusion.23
  280.0 2.5 copy_dynamic-update-slice_fusion.2
  282.6 2.9 gather_fusion
  285.5 2.1 fusion.23
  287.6 2.5 copy_dynamic-update-slice_fusion.2
  290.2 2.9 gather_fusion
  293.1 2.1 fusion.23
  295.2 2.6 copy_dynamic-update-slice_fusion.2
  297.9 2.9 gather_fusion
  300.8 2.1 fusion.23
  302.8 2.5 copy_dynamic-update-slice_fusion.2
  305.4 2.9 gather_fusion
  308.3 2.1 fusion.23
  310.4 2.5 copy_dynamic-update-slice_fusion.2
  313.0 2.9 gather_fusion
  315.9 2.1 fusion.23
  318.0 2.5 copy_dynamic-update-slice_fusion.2
  320.6 2.9 gather_fusion
  323.5 2.1 fusion.23
  325.6 2.5 copy_dynamic-update-slice_fusion.2
  328.2 2.9 gather_fusion
  333.2 2.5 copy_dynamic-update-slice_fusion.2
  335.8 2.9 gather_fusion
  338.7 2.1 fusion.23
  340.8 2.5 copy_dynamic-update-slice_fusion.2
  343.4 2.9 gather_fusion
  346.3 2.1 fusion.23
  348.4 2.5 copy_dynamic-update-slice_fusion.2
  351.0 2.9 gather_fusion
  353.9 2.1 fusion.23
  356.0 2.6 copy_dynamic-update-slice_fusion.2
  358.6 2.9 gather_fusion
  363.6 2.5 copy_dynamic-update-slice_fusion.2
  366.1 27.6 %reshape.24 = f32[8192,512]{1,0:T(8,128)} reshape(f32[128,64,8,64]{3,2,1,0:T(8,128)} %get-tuple-element.43) | data formatting | bytes 33554432 | tf_op jit(solution)/shard_map/reshape | solution.py:33
  393.8 344.0 %reduce-scatter.2.cloned.1.call-done = f32[1024,512]{1,0:T(8,128)} async-done(((f32[8192,512]{1,0:T(8,128)}), f32[1024,512]{1,0:T(8,128)}) %reduce-scatter.2.cloned.1.call-update) | async-done | bytes 2097168 | tf_op jit(solution)/shard_map/reduce_scatter | solution.py:34
  (57 shorter events, 7.8 us)
Async XLA Ops:
  6.5 2.3 copy-start
  6.5 61.4 %all-gather.6.cloned.1.call-start = ((), (), s32[]{:S(2)}) async-start(), calls=%async_computation.2 | async-start | bytes 2359296 | tf_op jit(solution)/shard_map/all_gather | solution.py:10
  7.3 184.1 %all-gather.8.cloned.1.call-start = ((), (), s32[]{:S(2)}) async-start(), calls=%async_computation.3 | async-start | bytes 17825792 | tf_op jit(solution)/shard_map/all_gather | solution.py:12
  8.0 240.6 %all-gather.4.cloned.1.call-start = ((), (), s32[]{:S(2)}) async-start(), calls=%async_computation.1 | async-start | bytes 4456448 | tf_op jit(solution)/shard_map/all_gather | solution.py:15
  8.7 729.0 %reduce-scatter.2.cloned.1.call-start = ((), (), s32[]{:S(2)}) async-start(), calls=%async_computation.4 | async-start | bytes 18874368 | tf_op jit(solution)/shard_map/reduce_scatter | solution.py:34
  393.7 344.0 %copy-start.1 = (s32[128,128]{1,0:T(8,128)S(1)}, s32[128,128]{1,0:T(8,128)}, u32[]{:S(2)}) copy-start(s32[128,128]{1,0:T(8,128)} %param.7) | copy-start | bytes 196612
Sparse Core Ops, SparseCore 0:
  8.9 59.0 all-gather.5
  70.2 121.1 all-gather.7
  193.9 54.6 all-gather.3
  393.9 343.8 reduce-scatter.1
where the time goes:
time: 748 us; the launch traced here: 744 us
  waiting for transfers between devices  571 us (76%)
  local copies, waits for them, and re-layouts  116 us (16%)
  matrix products  43.4 us (6%)
  between operations  13.1 us (2%)
    reduce_scatter x1, waiting for transfers between devices, local(): return lax.psum_scatter(flat, 'kr', scatter_dimension=0, tiled=True)  344 us
    all_gather x1, waiting for transfers between devices, local(): w_whole = lax.all_gather(screened, 'kc', axis=2, tiled=True)  123 us
    all_gather x1, waiting for transfers between devices, local(): column = lax.all_gather(densities, 'kr', axis=2, tiled=True)  59.1 us
    all_gather x1, waiting for transfers between devices, local(): row_dens = lax.all_gather(densities, 'kc', axis=0, tiled=True)  42.8 us
    gather x14, local copies, waits for them, and re-layouts, block_product(): chosen = screen_cols[q_block, picker]  40.5 us
    dynamic_update_slice x14, local copies, waits for them, and re-layouts, one_block(): lax.dynamic_update_slice_in_dim(kernel_slab, partial_value, row_block * b...  35.4 us
    dot_general x14, matrix products, block_product(): jnp.einsum('kpg,kjrg->kpjr', row_slice, chosen, preferred_element_type=jn...  29.1 us
    reshape x1, local copies, waits for them, and re-layouts, local(): flat = kernel_slab.reshape(k_total * pair_count, block_len * pair_count)  27.6 us
  transfers between devices with their start and end apart: 4, of which 4 were waited for; matrix products, arithmetic and copies ran while one was open for 2% of the time, Pallas kernels for 0%

commit v1 on v0

v1 whole, which is shorter than its diff:
```python
import functools

import jax
import jax.numpy as jnp
from jax import lax
from jax.experimental import pallas as pl
from jax.experimental.pallas import tpu as pltpu
from jax.sharding import PartitionSpec as P

MESH = pl.DeviceIdType.MESH
NT = (((1,), (1,)), ((), ()))
CHUNKS = 4
KINDS = 16


def kernel(d_ref, w_ref, q_ref, out_ref, wb, drow, dcol, dtmp, yb, psend, zrecv, xsend, xrecv, ssend, srecv,
           loc_sem, a_send, a_recv, d_send, d_recv, z_send, z_recv, x_send, x_recv, s_send, s_recv):
    r, c = lax.axis_index("kr"), lax.axis_index("kc")
    x, zl = r // 2, r % 2
    zh, y, core = c // 8, (c // 2) % 4, c % 2
    q_count = w_ref.shape[0]
    per = q_count // CHUNKS
    odd = core == 1
    vc = jnp.where(odd, 16 - c, c)
    swap_c = jnp.where(odd, 16 - c, c)

    def cid(zh_, y_, core_):
        return zh_ * 8 + y_ * 2 + core_

    yp, ym, y2, zo = (y + 1) % 4, (y + 3) % 4, (y + 2) % 4, 1 - zh
    up, down, across, sib = (r, cid(zh, yp, core)), (r, cid(zh, ym, core)), (r, cid(zo, y, core)), (r, cid(zh, y, 1 - core))

    def plane(i):
        return (r + i) % 8

    barrier = pltpu.get_barrier_semaphore()

    def greet(to):
        pl.semaphore_signal(barrier, inc=1, device_id=to, device_id_type=MESH)

    load_w = pltpu.make_async_copy(w_ref, wb.at[c], loc_sem.at[0])
    load_d = pltpu.make_async_copy(d_ref, drow.at[c], loc_sem.at[1])
    load_w.start()
    load_d.start()
    for to in (up, down, across, sib):
        greet(to)
    for i in range(1, 8):
        greet((plane(i), c))

    @pl.when(odd)
    def _():
        greet((r, swap_c))
        pl.semaphore_wait(barrier, 12)

    @pl.when(jnp.logical_not(odd))
    def _():
        pl.semaphore_wait(barrier, 11)

    load_d.wait()
    load_w.wait()

    def remote(src, dst, ssem, rsem, to):
        return pltpu.make_async_remote_copy(
            src_ref=src, dst_ref=dst, send_sem=ssem, recv_sem=rsem, device_id=to, device_id_type=MESH
        )

    swap_d = remote(drow.at[c], dtmp, d_send.at[0], d_recv.at[0], (r, swap_c))
    keep_d = pltpu.make_async_copy(drow.at[c], dtmp, loc_sem.at[2])

    @pl.when(odd)
    def _():
        swap_d.start()

    @pl.when(jnp.logical_not(odd))
    def _():
        keep_d.start()

    def part(s, who, half=None):
        if s < CHUNKS:
            if half is None:
                return wb.at[who, pl.ds(s * per, per)]
            return wb.at[who, pl.ds(s * per + half * (per // 2), per // 2)]
        if half is None:
            return drow.at[who]
        rows = drow.shape[1] // 2
        return drow.at[who, pl.ds(half * rows, rows)]

    sent = []

    def send(s, kind, who, to, recv_kind, half=None):
        ref = part(s, who, half)
        copy = remote(ref, ref, a_send.at[s, kind], a_recv.at[s, recv_kind], to)
        copy.start()
        sent.append(copy)

    def arrived(s, kind, who, half=None):
        ref = part(s, who, half)
        remote(ref, ref, a_send.at[s, kind], a_recv.at[s, kind], sib).wait_recv()

    c_ym, c_yp, c_y2 = cid(zh, ym, core), cid(zh, yp, core), cid(zh, y2, core)
    c_z, c_zym, c_zyp, c_zy2 = cid(zo, y, core), cid(zo, ym, core), cid(zo, yp, core), cid(zo, y2, core)
    blocks = [c, c_ym, c_yp, c_z, c_y2, c_zym, c_zyp, c_zy2]

    def own(s):
        send(s, 0, c, up, 0)
        send(s, 1, c, down, 1)
        send(s, 2, c, across, 2)
        send(s, 3, c, sib, 8)

    def relay_near(s):
        arrived(s, 0, c_ym)
        send(s, 4, c_ym, up, 3, 0)
        send(s, 5, c_ym, sib, 9)
        arrived(s, 1, c_yp)
        send(s, 6, c_yp, down, 4, 1)
        send(s, 7, c_yp, sib, 10)
        arrived(s, 2, c_z)
        send(s, 8, c_z, up, 5)
        send(s, 9, c_z, down, 6)
        send(s, 10, c_z, sib, 11)

    def relay_far(s):
        arrived(s, 3, c_y2, 0)
        arrived(s, 4, c_y2, 1)
        send(s, 11, c_y2, across, 7)
        send(s, 12, c_y2, sib, 12)

    def finish(s):
        arrived(s, 5, c_zym)
        send(s, 13, c_zym, sib, 13)
        arrived(s, 6, c_zyp)
        send(s, 14, c_zyp, sib, 14)
        arrived(s, 7, c_zy2)
        send(s, 15, c_zy2, sib, 15)
        for i, who in enumerate(blocks):
            arrived(s, 8 + i, who - core + (1 - core))

    def screen(s):
        def one(i, carry):
            q = s * per + i
            lhs = jnp.concatenate([dcol[j] for j in range(8)], axis=1)
            rhs = jnp.concatenate([wb[j, q] for j in range(16)], axis=1)
            yb[q] = lax.dot_general(lhs, rhs, NT, preferred_element_type=jnp.float32).astype(jnp.bfloat16)
            return carry

        lax.fori_loop(0, per, one, 0)

    for s in range(CHUNKS + 1):
        own(s)

    @pl.when(odd)
    def _():
        swap_d.wait()

    @pl.when(jnp.logical_not(odd))
    def _():
        keep_d.wait()

    col_copies = []
    for i in range(1, 8):
        copy = remote(dtmp, dcol.at[r], d_send.at[i], d_recv.at[i], (plane(i), c))
        copy.start()
        col_copies.append(copy)
    col_own = pltpu.make_async_copy(dtmp, dcol.at[r], loc_sem.at[3])
    col_own.start()

    relay_near(0)
    relay_near(1)
    relay_far(0)
    relay_near(2)
    relay_far(1)
    finish(0)
    col_own.wait()
    for i in range(1, 8):
        src = dcol.at[(r + 8 - i) % 8]
        remote(src, src, d_send.at[i], d_recv.at[i], sib).wait_recv()
    screen(0)
    relay_near(3)
    relay_far(2)
    finish(1)
    screen(1)
    relay_near(4)
    relay_far(3)
    finish(2)
    screen(2)
    relay_far(4)
    finish(3)
    screen(3)
    finish(4)

    def product(b, k):
        rhs = jnp.concatenate(
            [yb[q_ref[b * 8 + k, vc * 8 + j], pl.ds(j * 64, 64), :] for j in range(8)], axis=0
        )
        lhs = drow[b, pl.ds(k * 64, 64), :]
        return lax.dot_general(lhs, rhs, NT, preferred_element_type=jnp.float32)

    partner = (r - zl + (1 - zl), c)

    def row_block(t, zl_):
        x_to = (x + 1 + t // 2) % 4
        return 2 * (2 * x_to + zl_) + t % 2

    def z_copy(t):
        return remote(psend.at[t], zrecv.at[t], z_send.at[t], z_recv.at[t], partner)

    def to_partner(t, carry):
        b = row_block(t, 1 - zl)

        @pl.when(b <= vc)
        def _():
            for k in range(8):
                psend[t, pl.ds(k * 64, 64), :] = product(b, k).astype(jnp.bfloat16)
            z_copy(t).start()

        return carry

    lax.fori_loop(0, 8, to_partner, 0)

    def x_copy(t):
        x_to = (x + 1 + t // 2) % 4
        return remote(xsend.at[t], xrecv.at[t], x_send.at[t], x_recv.at[t], (2 * x_to + zl, c))

    def along_x(t, carry):
        b = row_block(t, zl)

        @pl.when(b <= vc)
        def _():
            z_copy(t).wait_recv()
            for k in range(8):
                rows = pl.ds(k * 64, 64)
                xsend[t, rows, :] = (product(b, k) + zrecv[t, rows, :].astype(jnp.float32)).astype(jnp.bfloat16)
            x_copy(t).start()

        return carry

    lax.fori_loop(0, 6, along_x, 0)

    def s_copy(i):
        return remote(ssend.at[i], srecv.at[i], s_send.at[i], s_recv.at[i], (r, swap_c))

    for i in range(2):
        b = 2 * r + i
        t = 6 + i

        @pl.when(b <= vc)
        def _():
            z_copy(t).wait_recv()
            for k in range(8):
                out_ref[pl.ds(i * 512 + k * 64, 64), :] = product(b, k) + zrecv[t, pl.ds(k * 64, 64), :].astype(jnp.float32)
            for e in range(3):
                x_copy(2 * e + i).wait_recv()

            @pl.when(odd)
            def _():
                for k in range(8):
                    rows = pl.ds(k * 64, 64)
                    total = out_ref[pl.ds(i * 512 + k * 64, 64), :]
                    for e in range(3):
                        total = total + xrecv[2 * e + i, rows, :].astype(jnp.float32)
                    ssend[i, rows, :] = total.astype(jnp.bfloat16)
                s_copy(i).start()

            @pl.when(jnp.logical_not(odd))
            def _():
                for k in range(8):
                    rows = pl.ds(k * 64, 64)
                    total = out_ref[pl.ds(i * 512 + k * 64, 64), :]
                    for e in range(3):
                        total = total + xrecv[2 * e + i, rows, :].astype(jnp.float32)
                    out_ref[pl.ds(i * 512 + k * 64, 64), :] = total

    for i in range(2):
        b = 2 * r + i

        @pl.when(b > c)
        def _():
            out_ref[pl.ds(i * 512, 512), :] = jnp.zeros((512, 512), jnp.float32)

        @pl.when(jnp.logical_and(odd, b <= c))
        def _():
            s_copy(i).wait_recv()
            out_ref[pl.ds(i * 512, 512), :] = srecv[i].astype(jnp.float32)

    for copy in sent + col_copies:
        copy.wait_send()

    def drain_z(t, carry):
        @pl.when(row_block(t, 1 - zl) <= vc)
        def _():
            z_copy(t).wait_send()

        return carry

    lax.fori_loop(0, 8, drain_z, 0)

    def drain_x(t, carry):
        @pl.when(row_block(t, zl) <= vc)
        def _():
            x_copy(t).wait_send()

        return carry

    lax.fori_loop(0, 6, drain_x, 0)
    for i in range(2):
        @pl.when(jnp.logical_and(odd, 2 * r + i <= vc))
        def _():
            s_copy(i).wait_send()


def local(densities, screened, q_table):
    block_len, pair_count, g_slice = densities.shape
    d = densities.reshape(block_len * pair_count, g_slice)
    bf = jnp.bfloat16
    dma = pltpu.SemaphoreType.DMA
    return pl.pallas_call(
        kernel,
        out_shape=jax.ShapeDtypeStruct((1024, 512), jnp.float32),
        in_specs=[
            pl.BlockSpec(memory_space=pl.ANY),
            pl.BlockSpec(memory_space=pl.ANY),
            pl.BlockSpec(memory_space=pltpu.SMEM),
        ],
        out_specs=pl.BlockSpec(memory_space=pltpu.VMEM),
        scratch_shapes=[
            pltpu.VMEM((16, 16, 256, 128), bf),
            pltpu.VMEM((16, 512, 256), bf),
            pltpu.VMEM((8, 512, 256), bf),
            pltpu.VMEM((512, 256), bf),
            pltpu.VMEM((16, 512, 256), bf),
            pltpu.VMEM((8, 512, 512), bf),
            pltpu.VMEM((8, 512, 512), bf),
            pltpu.VMEM((6, 512, 512), bf),
            pltpu.VMEM((6, 512, 512), bf),
            pltpu.VMEM((2, 512, 512), bf),
            pltpu.VMEM((2, 512, 512), bf),
            dma((4,)),
            dma((CHUNKS + 1, KINDS)),
            dma((CHUNKS + 1, KINDS)),
            dma((8,)),
            dma((8,)),
            dma((8,)),
            dma((8,)),
            dma((6,)),
            dma((6,)),
            dma((2,)),
            dma((2,)),
        ],
        compiler_params=pltpu.CompilerParams(
            collective_id=0, has_side_effects=True, vmem_limit_bytes=60 * 2**20
        ),
        cost_estimate=pl.CostEstimate(flops=10 * 10**9, bytes_accessed=4 * 2**20, transcendentals=0),
    )(d, screened, q_table)


def solution(mesh):
    return jax.shard_map(
        local,
        mesh=mesh,
        in_specs=(P("kc", None, "kr"), P(None, "kr", "kc"), P()),
        out_specs=P("kr", "kc"),
        check_vma=False,
    )
```

time: 748 us -> 195 us (0.26)
  the two profiles are of different devices: /device:TPU:81 before, /device:TPU:67 now
where the time goes in v1:
time: 195 us
  Pallas kernels  192 us (98%)
  local copies, waits for them, and re-layouts  3.08 us (2%)
    pallas_call x1, Pallas kernels, local(): pl.pallas_call(kernel, out_shape=jax.ShapeDtypeStruct((1024, 512), jnp.fl...  192 us

profile of v1, /device:TPU:67, one launch (start us, length us, event | category | flops | bytes accessed | tf_op | source)
XLA Modules:
  0.0 195.1 jit_solution(5255176318223841587)
XLA Ops:
  0.0 192.0 %shard_map.37 = f32[1024,512]{1,0:T(8,128)} custom-call(bf16[512,256]{1,0:T(8,128)(2,1)} %bitcast.1, bf16[16,256,128]{2,1,0:T(8,128)(2,1)} %w_ref.1, s32[128,128]{1,0:T(8,128)} %q_ref.1), custom_call_target="tpu_custom_call" | custom-call | flops 10000000000 | bytes 4194304 | tf_op jit(solution)/shard_map/pallas_call | solution.py:316
  192.1 3.1 %copy.5 = f32[1024,512]{1,0:T(8,128)} copy(f32[1024,512]{1,0:T(8,128)} %shard_map.37) | data formatting | bytes 4194304

commit v2 on v1

v2 whole, which is shorter than its diff:
```python
import functools

import jax
import jax.numpy as jnp
from jax import lax
from jax.experimental import pallas as pl
from jax.experimental.pallas import tpu as pltpu
from jax.sharding import PartitionSpec as P

MESH = pl.DeviceIdType.MESH
NT = (((1,), (1,)), ((), ()))
CHUNKS = 4
KINDS = 16
AX, AZ, BZ, BX, BS, ITEMS = 0, 12, 16, 24, 30, 32


def kernel(d_ref, w_ref, q_ref, out_ref, wb, drow, dcol, dtmp, yb, pout, pin,
           loc_sem, a_send, a_recv, d_send, d_recv, p_send, p_recv):
    r, c = lax.axis_index("kr"), lax.axis_index("kc")
    x, zl = r // 2, r % 2
    zh, y, core = c // 8, (c // 2) % 4, c % 2
    q_count = w_ref.shape[0]
    per = q_count // CHUNKS
    odd = core == 1
    vc = jnp.where(odd, 16 - c, c)
    swap_c = jnp.where(odd, 16 - c, c)

    def cid(zh_, y_, core_):
        return zh_ * 8 + y_ * 2 + core_

    yp, ym, y2, zo = (y + 1) % 4, (y + 3) % 4, (y + 2) % 4, 1 - zh
    up, down, across, sib = (r, cid(zh, yp, core)), (r, cid(zh, ym, core)), (r, cid(zo, y, core)), (r, cid(zh, y, 1 - core))

    partner = (2 * x + 1 - zl, c)

    def along(i):
        return 2 * ((x + i) % 4) + zl

    barrier = pltpu.get_barrier_semaphore()

    def greet(to):
        pl.semaphore_signal(barrier, inc=1, device_id=to, device_id_type=MESH)

    load_w = pltpu.make_async_copy(w_ref, wb.at[c], loc_sem.at[0])
    load_d = pltpu.make_async_copy(d_ref, drow.at[c], loc_sem.at[1])
    load_w.start()
    load_d.start()
    for to in (up, down, across, sib, partner):
        greet(to)
    for i in range(1, 4):
        greet((along(i), c))

    @pl.when(odd)
    def _():
        greet((r, swap_c))
        greet((partner[0], swap_c))
        pl.semaphore_wait(barrier, 10)

    @pl.when(jnp.logical_not(odd))
    def _():
        pl.semaphore_wait(barrier, 8)

    load_d.wait()
    load_w.wait()

    def remote(src, dst, ssem, rsem, to):
        return pltpu.make_async_remote_copy(
            src_ref=src, dst_ref=dst, send_sem=ssem, recv_sem=rsem, device_id=to, device_id_type=MESH
        )

    swap_d = remote(drow.at[c], dtmp, d_send.at[7], d_recv.at[7], (r, swap_c))
    keep_d = pltpu.make_async_copy(drow.at[c], dtmp, loc_sem.at[2])

    @pl.when(odd)
    def _():
        swap_d.start()

    @pl.when(jnp.logical_not(odd))
    def _():
        keep_d.start()

    def part(s, who, half=None):
        if s < CHUNKS:
            if half is None:
                return wb.at[who, pl.ds(s * per, per)]
            return wb.at[who, pl.ds(s * per + half * (per // 2), per // 2)]
        if half is None:
            return drow.at[who]
        rows = drow.shape[1] // 2
        return drow.at[who, pl.ds(half * rows, rows)]

    sent = []

    def send(s, kind, who, to, recv_kind, half=None):
        ref = part(s, who, half)
        copy = remote(ref, ref, a_send.at[s, kind], a_recv.at[s, recv_kind], to)
        copy.start()
        sent.append(copy)

    def arrived(s, kind, who, half=None):
        ref = part(s, who, half)
        remote(ref, ref, a_send.at[s, kind], a_recv.at[s, kind], sib).wait_recv()

    c_ym, c_yp, c_y2 = cid(zh, ym, core), cid(zh, yp, core), cid(zh, y2, core)
    c_z, c_zym, c_zyp, c_zy2 = cid(zo, y, core), cid(zo, ym, core), cid(zo, yp, core), cid(zo, y2, core)
    blocks = [c, c_ym, c_yp, c_z, c_y2, c_zym, c_zyp, c_zy2]

    def own(s):
        send(s, 0, c, up, 0)
        send(s, 1, c, down, 1)
        send(s, 2, c, across, 2)
        send(s, 3, c, sib, 8)

    def relay_near(s):
        arrived(s, 0, c_ym)
        send(s, 4, c_ym, up, 3, 0)
        send(s, 5, c_ym, sib, 9)
        arrived(s, 1, c_yp)
        send(s, 6, c_yp, down, 4, 1)
        send(s, 7, c_yp, sib, 10)
        arrived(s, 2, c_z)
        send(s, 8, c_z, up, 5)
        send(s, 9, c_z, down, 6)
        send(s, 10, c_z, sib, 11)

    def relay_far(s):
        arrived(s, 3, c_y2, 0)
        arrived(s, 4, c_y2, 1)
        send(s, 11, c_y2, across, 7)
        send(s, 12, c_y2, sib, 12)

    def finish(s):
        arrived(s, 5, c_zym)
        send(s, 13, c_zym, sib, 13)
        arrived(s, 6, c_zyp)
        send(s, 14, c_zyp, sib, 14)
        arrived(s, 7, c_zy2)
        send(s, 15, c_zy2, sib, 15)
        for i, who in enumerate(blocks):
            arrived(s, 8 + i, who - core + (1 - core))

    def screen(s):
        def one(i, carry):
            q = s * per + i
            lhs = jnp.concatenate([dcol[j] for j in range(8)], axis=1)
            rhs = jnp.concatenate([wb[j, q] for j in range(16)], axis=1)
            yb[q] = lax.dot_general(lhs, rhs, NT, preferred_element_type=jnp.float32).astype(jnp.bfloat16)
            return carry

        lax.fori_loop(0, per, one, 0)

    for s in range(CHUNKS + 1):
        own(s)

    @pl.when(odd)
    def _():
        swap_d.wait()

    @pl.when(jnp.logical_not(odd))
    def _():
        keep_d.wait()

    col_copies = []

    def col_send(i, src, who, to):
        copy = remote(src, dcol.at[who], d_send.at[i], d_recv.at[i], to)
        copy.start()
        col_copies.append(copy)

    def col_arrived(i, who):
        src = dcol.at[who]
        remote(src, src, d_send.at[i], d_recv.at[i], sib).wait_recv()

    col_send(0, dtmp, r, partner)
    for i in range(1, 4):
        col_send(i, dtmp, r, (along(i), c))
    col_own = pltpu.make_async_copy(dtmp, dcol.at[r], loc_sem.at[3])
    col_own.start()

    col_arrived(0, partner[0])
    for i in range(1, 4):
        col_send(3 + i, dcol.at[partner[0]], partner[0], (along(i), c))
    relay_near(0)
    relay_near(1)
    relay_far(0)
    relay_near(2)
    relay_far(1)
    finish(0)
    col_own.wait()
    for i in range(1, 4):
        col_arrived(i, along(4 - i))
        col_arrived(3 + i, 2 * ((x + 4 - i) % 4) + 1 - zl)
    screen(0)
    relay_near(3)
    relay_far(2)
    finish(1)
    screen(1)
    relay_near(4)
    relay_far(3)
    finish(2)
    screen(2)
    relay_far(4)
    finish(3)
    screen(3)
    finish(4)

    def product(b, k, half):
        rhs = jnp.concatenate(
            [yb[q_ref[b * 8 + k, vc * 8 + j], pl.ds(j * 64, 64), :] for j in range(4 * half, 4 * half + 4)], axis=0
        )
        lhs = drow[b, pl.ds(k * 64, 64), :]
        return lax.dot_general(lhs, rhs, NT, preferred_element_type=jnp.float32)

    step = 1 - 2 * (x % 2)
    x_far, x_pair, x_next = (x + 2) % 4, (x + 4 + step) % 4, (x + 4 - step) % 4
    to_pair, to_next = (2 * x_pair + zl, c), (2 * x_next + zl, c)
    dest = [x_far, x_pair, x_next, x]

    def a_row(role, i):
        return 4 * dest[role] + i

    def b_row(role, i, zl_):
        return 4 * dest[role] + 2 * zl_ + i

    def item(base, i, to):
        return remote(pout.at[base + i], pin.at[base + i], p_send.at[base + i], p_recv.at[base + i], to)

    def fill(base, i, b, half, adds):
        for k in range(8):
            rows = pl.ds(k * 64, 64)
            value = product(b, k, half)
            for add in adds:
                value = value + pin[add, rows, :].astype(jnp.float32)
            pout[base + i, rows, :] = value.astype(jnp.bfloat16)

    def each(count, row, body):
        def one(i, carry):
            b = row(i)

            @pl.when(b <= vc)
            def _():
                body(i, b)

            return carry

        lax.fori_loop(0, count, one, 0)

    def a_first(role):
        def body(i, b):
            fill(AX + 4 * role, i, b, 1, [])
            item(AX + 4 * role, i, to_pair).start()

        each(4, lambda i: a_row(role, i), body)

    def a_mid():
        def body(i, b):
            item(AX, i, to_pair).wait_recv()
            fill(AX + 8, i, b, 1, [AX + i])
            item(AX + 8, i, to_next).start()

        each(4, lambda i: a_row(2, i), body)

    def b_across(role):
        def body(i, b):
            fill(BZ + 2 * role, i, b, 0, [])
            item(BZ + 2 * role, i, partner).start()

        each(2, lambda i: b_row(role, i, 1 - zl), body)

    def b_first(role):
        def body(i, b):
            item(BZ + 2 * role, i, partner).wait_recv()
            fill(BX + 2 * role, i, b, 0, [BZ + 2 * role + i])
            item(BX + 2 * role, i, to_pair).start()

        each(2, lambda i: b_row(role, i, zl), body)

    def b_mid():
        def body(i, b):
            item(BZ + 4, i, partner).wait_recv()
            item(BX, i, to_pair).wait_recv()
            fill(BX + 4, i, b, 0, [BZ + 4 + i, BX + i])
            item(BX + 4, i, to_next).start()

        each(2, lambda i: b_row(2, i, zl), body)

    even = jnp.logical_not(odd)

    def a_home(z_from, z_to, i):
        slot = AZ + 2 * z_from + i
        to = (2 * x + z_to, swap_c)
        return remote(pout.at[AZ + 2 * z_to + i], pin.at[slot], p_send.at[AZ + 2 * z_to + i], p_recv.at[slot], to)

    def a_final(z_to, is_own):
        def body(i, b):
            item(AX + 4, 2 * z_to + i, to_pair).wait_recv()
            item(AX + 8, 2 * z_to + i, to_next).wait_recv()
            adds = [AX + 4 + 2 * z_to + i, AX + 8 + 2 * z_to + i]
            for k in range(8):
                rows = pl.ds(k * 64, 64)
                value = product(b, k, 1)
                for add in adds:
                    value = value + pin[add, rows, :].astype(jnp.float32)
                if is_own:
                    out_ref[pl.ds(i * 512 + k * 64, 64), 256:] = value
                pout[AZ + 2 * z_to + i, rows, :] = value.astype(jnp.bfloat16)

            @pl.when(odd)
            def _():
                a_home(zl, z_to, i).start()

            if not is_own:
                @pl.when(even)
                def _():
                    a_home(zl, z_to, i).start()

        each(2, lambda i: 4 * x + 2 * z_to + i, body)

    def b_home(i):
        return item(BS, i, (r, swap_c))

    def b_final():
        def body(i, b):
            item(BZ + 6, i, partner).wait_recv()
            item(BX + 2, i, to_pair).wait_recv()
            item(BX + 4, i, to_next).wait_recv()
            for k in range(8):
                rows = pl.ds(k * 64, 64)
                value = product(b, k, 0)
                for add in (BZ + 6 + i, BX + 2 + i, BX + 4 + i):
                    value = value + pin[add, rows, :].astype(jnp.float32)
                out_ref[pl.ds(i * 512 + k * 64, 64), :256] = value
                pout[BS + i, rows, :] = value.astype(jnp.bfloat16)

            @pl.when(odd)
            def _():
                b_home(i).start()

        each(2, lambda i: 4 * x + 2 * zl + i, body)

    b_across(0)
    a_first(0)
    b_across(1)
    a_first(1)
    b_across(2)
    b_across(3)
    b_first(0)
    a_mid()
    b_first(1)
    b_mid()
    a_final(1 - zl, False)
    a_final(zl, True)
    b_final()

    for i in range(2):
        b = 2 * r + i
        rows = pl.ds(i * 512, 512)

        @pl.when(b > c)
        def _():
            out_ref[rows, :] = jnp.zeros((512, 512), jnp.float32)

        @pl.when(jnp.logical_and(even, b <= c))
        def _():
            a_home(1 - zl, zl, i).wait_recv()
            out_ref[rows, 256:] = out_ref[rows, 256:] + pin[AZ + 2 * (1 - zl) + i].astype(jnp.float32)

        @pl.when(jnp.logical_and(odd, b <= c))
        def _():
            a_home(0, zl, i).wait_recv()
            a_home(1, zl, i).wait_recv()
            out_ref[rows, 256:] = pin[AZ + i].astype(jnp.float32) + pin[AZ + 2 + i].astype(jnp.float32)
            b_home(i).wait_recv()
            out_ref[rows, :256] = pin[BS + i].astype(jnp.float32)

    for copy in sent + col_copies:
        copy.wait_send()

    def left(count, row, copy, when=None):
        def one(i, carry):
            live = row(i) <= vc
            if when is not None:
                live = jnp.logical_and(live, when)

            @pl.when(live)
            def _():
                copy(i).wait_send()

            return carry

        lax.fori_loop(0, count, one, 0)

    for role in range(3):
        left(4, lambda i: a_row(role, i), lambda i: item(AX + 4 * role, i, to_pair))
        left(2, lambda i: b_row(role, i, zl), lambda i: item(BX + 2 * role, i, to_pair))
    for role in range(4):
        left(2, lambda i: b_row(role, i, 1 - zl), lambda i: item(BZ + 2 * role, i, partner))
    left(2, lambda i: 4 * x + 2 * (1 - zl) + i, lambda i: a_home(zl, 1 - zl, i))
    left(2, lambda i: 4 * x + 2 * zl + i, lambda i: a_home(zl, zl, i), odd)
    left(2, lambda i: 4 * x + 2 * zl + i, b_home, odd)


def local(densities, screened, q_table):
    block_len, pair_count, g_slice = densities.shape
    d = densities.reshape(block_len * pair_count, g_slice)
    bf = jnp.bfloat16
    dma = pltpu.SemaphoreType.DMA
    return pl.pallas_call(
        kernel,
        out_shape=jax.ShapeDtypeStruct((1024, 512), jnp.float32),
        in_specs=[
            pl.BlockSpec(memory_space=pl.ANY),
            pl.BlockSpec(memory_space=pl.ANY),
            pl.BlockSpec(memory_space=pltpu.SMEM),
        ],
        out_specs=pl.BlockSpec(memory_space=pltpu.VMEM),
        scratch_shapes=[
            pltpu.VMEM((16, 16, 256, 128), bf),
            pltpu.VMEM((16, 512, 256), bf),
            pltpu.VMEM((8, 512, 256), bf),
            pltpu.VMEM((512, 256), bf),
            pltpu.VMEM((16, 512, 256), bf),
            pltpu.VMEM((ITEMS, 512, 256), bf),
            pltpu.VMEM((ITEMS, 512, 256), bf),
            dma((4,)),
            dma((CHUNKS + 1, KINDS)),
            dma((CHUNKS + 1, KINDS)),
            dma((8,)),
            dma((8,)),
            dma((ITEMS,)),
            dma((ITEMS,)),
        ],
        compiler_params=pltpu.CompilerParams(
            collective_id=0, has_side_effects=True, vmem_limit_bytes=60 * 2**20
        ),
        cost_estimate=pl.CostEstimate(flops=10 * 10**9, bytes_accessed=4 * 2**20, transcendentals=0),
    )(d, screened, q_table)


def solution(mesh):
    return jax.shard_map(
        local,
        mesh=mesh,
        in_specs=(P("kc", None, "kr"), P(None, "kr", "kc"), P()),
        out_specs=P("kr", "kc"),
        check_vma=False,
    )
```

time: 195 us -> 162 us (0.83)
  the two profiles are of different devices: /device:TPU:67 before, /device:TPU:81 now
where the time goes in v2:
time: 162 us
  Pallas kernels  159 us (98%)
  local copies, waits for them, and re-layouts  3.08 us (2%)
    pallas_call x1, Pallas kernels, local(): pl.pallas_call(kernel, out_shape=jax.ShapeDtypeStruct((1024, 512), jnp.fl...  159 us

profile of v2, /device:TPU:81, one launch (start us, length us, event | category | flops | bytes accessed | tf_op | source)
XLA Modules:
  0.0 162.2 jit_solution(9315723689954145218)
XLA Ops:
  0.0 159.1 %shard_map.37 = f32[1024,512]{1,0:T(8,128)} custom-call(bf16[512,256]{1,0:T(8,128)(2,1)} %bitcast.1, bf16[16,256,128]{2,1,0:T(8,128)(2,1)} %w_ref.1, s32[128,128]{1,0:T(8,128)} %q_ref.1), custom_call_target="tpu_custom_call" | custom-call | flops 10000000000 | bytes 4194304 | tf_op jit(solution)/shard_map/pallas_call | solution.py:408
  159.1 3.1 %copy.5 = f32[1024,512]{1,0:T(8,128)} copy(f32[1024,512]{1,0:T(8,128)} %shard_map.37) | data formatting | bytes 4194304

commit v3 on v2

--- a/solution.py
+++ b/solution.py
@@ -10,11 +10,12 @@
 MESH = pl.DeviceIdType.MESH
 NT = (((1,), (1,)), ((), ()))
 CHUNKS = 4
-KINDS = 16
+AHEAD = 2
+KINDS = 17
 AX, AZ, BZ, BX, BS, ITEMS = 0, 12, 16, 24, 30, 32
 
 
-def kernel(d_ref, w_ref, q_ref, out_ref, wb, drow, dcol, dtmp, yb, pout, pin,
+def kernel(d_ref, w_ref, q_hbm, out_ref, q_ref, wb, drow, dcol, dtmp, yb, pout, pin,
            loc_sem, a_send, a_recv, d_send, d_recv, p_send, p_recv):
     r, c = lax.axis_index("kr"), lax.axis_index("kc")
     x, zl = r // 2, r % 2
@@ -43,8 +44,10 @@
 
     load_w = pltpu.make_async_copy(w_ref, wb.at[c], loc_sem.at[0])
     load_d = pltpu.make_async_copy(d_ref, drow.at[c], loc_sem.at[1])
+    load_q = pltpu.make_async_copy(q_hbm, q_ref, loc_sem.at[4])
     load_w.start()
     load_d.start()
+    load_q.start()
     for to in (up, down, across, sib, partner):
         greet(to)
     for i in range(1, 4):
@@ -95,7 +98,8 @@
         ref = part(s, who, half)
         copy = remote(ref, ref, a_send.at[s, kind], a_recv.at[s, recv_kind], to)
         copy.start()
-        sent.append(copy)
+        if s < CHUNKS:
+            sent.append(copy)
 
     def arrived(s, kind, who, half=None):
         ref = part(s, who, half)
@@ -114,10 +118,12 @@
     def relay_near(s):
         arrived(s, 0, c_ym)
         send(s, 4, c_ym, up, 3, 0)
-        send(s, 5, c_ym, sib, 9)
         arrived(s, 1, c_yp)
         send(s, 6, c_yp, down, 4, 1)
+        send(s, 5, c_ym, sib, 9)
         send(s, 7, c_yp, sib, 10)
+
+    def relay_across(s):
         arrived(s, 2, c_z)
         send(s, 8, c_z, up, 5)
         send(s, 9, c_z, down, 6)
@@ -139,6 +145,45 @@
         for i, who in enumerate(blocks):
             arrived(s, 8 + i, who - core + (1 - core))
 
+    rows_at = CHUNKS
+
+    def near_out():
+        send(rows_at, 0, c, up, 0)
+        send(rows_at, 1, c, down, 1)
+        send(rows_at, 3, c, sib, 8)
+
+    def near_on():
+        relay_near(rows_at)
+
+    def near_end():
+        arrived(rows_at, 3, c_y2, 0)
+        arrived(rows_at, 4, c_y2, 1)
+        send(rows_at, 12, c_y2, sib, 12)
+        for i in (0, 1, 2, 4):
+            arrived(rows_at, 8 + i, blocks[i] - core + (1 - core))
+
+    def cross_out():
+        relay_across(rows_at)
+
+    def cross_on():
+        arrived(rows_at, 5, c_zym)
+        send(rows_at, 11, c_zym, up, 7, 0)
+        arrived(rows_at, 6, c_zyp)
+        send(rows_at, 16, c_zyp, down, 16, 1)
+        send(rows_at, 13, c_zym, sib, 13)
+        send(rows_at, 14, c_zyp, sib, 14)
+
+    def cross_end():
+        arrived(rows_at, 7, c_zy2, 0)
+        arrived(rows_at, 16, c_zy2, 1)
+        send(rows_at, 15, c_zy2, sib, 15)
+        for i in (3, 5, 6, 7):
+            arrived(rows_at, 8 + i, blocks[i] - core + (1 - core))
+
+    def rows_step(near, cross, lower):
+        pl.when(zh == (0 if lower else 1))(near)
+        pl.when(zh == (1 if lower else 0))(cross)
+
     def screen(s):
         def one(i, carry):
             q = s * per + i
@@ -149,7 +194,7 @@
 
         lax.fori_loop(0, per, one, 0)
 
-    for s in range(CHUNKS + 1):
+    for s in range(AHEAD):
         own(s)
 
     @pl.when(odd)
@@ -180,29 +225,34 @@
     col_arrived(0, partner[0])
     for i in range(1, 4):
         col_send(3 + i, dcol.at[partner[0]], partner[0], (along(i), c))
-    relay_near(0)
-    relay_near(1)
-    relay_far(0)
-    relay_near(2)
-    relay_far(1)
-    finish(0)
+    for s in range(CHUNKS):
+        relay_near(s)
+        if s + AHEAD < CHUNKS:
+            own(s + AHEAD)
+        elif s + AHEAD == CHUNKS:
+            send(rows_at, 2, c, across, 2)
+            pl.when(zh == 0)(near_out)
+        if s >= 1:
+            relay_far(s - 1)
+    relay_across(0)
+    relay_far(CHUNKS - 1)
+    rows_step(near_on, cross_out, True)
+    for s in range(1, CHUNKS):
+        relay_across(s)
     col_own.wait()
     for i in range(1, 4):
         col_arrived(i, along(4 - i))
         col_arrived(3 + i, 2 * ((x + 4 - i) % 4) + 1 - zl)
-    screen(0)
-    relay_near(3)
-    relay_far(2)
-    finish(1)
-    screen(1)
-    relay_near(4)
-    relay_far(3)
-    finish(2)
-    screen(2)
-    relay_far(4)
-    finish(3)
-    screen(3)
-    finish(4)
+    for s in range(CHUNKS - 1):
+        finish(s)
+        if s == 0:
+            rows_step(lambda: None, cross_on, True)
+        screen(s)
+    rows_step(near_end, cross_end, True)
+    finish(CHUNKS - 1)
+    rows_step(near_out, cross_out, False)
+    load_q.wait()
+    screen(CHUNKS - 1)
 
     def product(b, k, half):
         rhs = jnp.concatenate(
@@ -217,7 +267,8 @@
     dest = [x_far, x_pair, x_next, x]
 
     def a_row(role, i):
-        return 4 * dest[role] + i
+        to = dest[role] if isinstance(role, int) else jnp.where(role == 0, x_far, x_pair)
+        return 4 * to + i
 
     def b_row(role, i, zl_):
         return 4 * dest[role] + 2 * zl_ + i
@@ -260,12 +311,19 @@
 
         each(4, lambda i: a_row(2, i), body)
 
-    def b_across(role):
-        def body(i, b):
-            fill(BZ + 2 * role, i, b, 0, [])
-            item(BZ + 2 * role, i, partner).start()
-
-        each(2, lambda i: b_row(role, i, 1 - zl), body)
+    zk = jnp.where(odd, 1 - zl, zl)
+
+    def b_slot(to):
+        return BZ + 2 * jnp.where(to == x_far, 0, jnp.where(to == x_pair, 1, jnp.where(to == x_next, 2, 3)))
+
+    def b_across(to):
+        base = b_slot(to)
+
+        def body(i, b):
+            fill(base, i, b, 0, [])
+            item(base, i, partner).start()
+
+        each(2, lambda i: 4 * to + 2 * (1 - zk) + i, body)
 
     def b_first(role):
         def body(i, b):
@@ -273,7 +331,7 @@
             fill(BX + 2 * role, i, b, 0, [BZ + 2 * role + i])
             item(BX + 2 * role, i, to_pair).start()
 
-        each(2, lambda i: b_row(role, i, zl), body)
+        each(2, lambda i: b_row(role, i, zk), body)
 
     def b_mid():
         def body(i, b):
@@ -282,7 +340,7 @@
             fill(BX + 4, i, b, 0, [BZ + 4 + i, BX + i])
             item(BX + 4, i, to_next).start()
 
-        each(2, lambda i: b_row(2, i, zl), body)
+        each(2, lambda i: b_row(2, i, zk), body)
 
     even = jnp.logical_not(odd)
 
@@ -317,7 +375,7 @@
         each(2, lambda i: 4 * x + 2 * z_to + i, body)
 
     def b_home(i):
-        return item(BS, i, (r, swap_c))
+        return item(BS, i, (2 * x + zk, swap_c))
 
     def b_final():
         def body(i, b):
@@ -336,20 +394,24 @@
             def _():
                 b_home(i).start()
 
-        each(2, lambda i: 4 * x + 2 * zl + i, body)
-
+        each(2, lambda i: 4 * x + 2 * zk + i, body)
+
+    low_first = jnp.where(x >= 2, 0, 1)
+    a_first(low_first)
     b_across(0)
-    a_first(0)
     b_across(1)
-    a_first(1)
+    rows_step(near_on, cross_on, False)
+    rows_step(near_end, cross_end, False)
+    pl.when(x < 2)(lambda: a_first(0))
     b_across(2)
     b_across(3)
+    a_mid()
+    pl.when(x >= 2)(lambda: a_first(1))
     b_first(0)
-    a_mid()
     b_first(1)
+    a_final(zl, True)
+    a_final(1 - zl, False)
     b_mid()
-    a_final(1 - zl, False)
-    a_final(zl, True)
     b_final()
 
     for i in range(2):
@@ -375,6 +437,9 @@
 
     for copy in sent + col_copies:
         copy.wait_send()
+    for kind in range(KINDS):
+        ref = part(rows_at, c, 0 if kind in (4, 6, 11, 16) else None)
+        remote(ref, ref, a_send.at[rows_at, kind], a_recv.at[rows_at, kind], sib).wait_send()
 
     def left(count, row, copy, when=None):
         def one(i, carry):
@@ -392,12 +457,12 @@
 
     for role in range(3):
         left(4, lambda i: a_row(role, i), lambda i: item(AX + 4 * role, i, to_pair))
-        left(2, lambda i: b_row(role, i, zl), lambda i: item(BX + 2 * role, i, to_pair))
+        left(2, lambda i: b_row(role, i, zk), lambda i: item(BX + 2 * role, i, to_pair))
     for role in range(4):
-        left(2, lambda i: b_row(role, i, 1 - zl), lambda i: item(BZ + 2 * role, i, partner))
+        left(2, lambda i: b_row(role, i, 1 - zk), lambda i: item(BZ + 2 * role, i, partner))
     left(2, lambda i: 4 * x + 2 * (1 - zl) + i, lambda i: a_home(zl, 1 - zl, i))
     left(2, lambda i: 4 * x + 2 * zl + i, lambda i: a_home(zl, zl, i), odd)
-    left(2, lambda i: 4 * x + 2 * zl + i, b_home, odd)
+    left(2, lambda i: 4 * x + 2 * zk + i, b_home, odd)
 
 
 def local(densities, screened, q_table):
@@ -411,10 +476,11 @@
         in_specs=[
             pl.BlockSpec(memory_space=pl.ANY),
             pl.BlockSpec(memory_space=pl.ANY),
-            pl.BlockSpec(memory_space=pltpu.SMEM),
+            pl.BlockSpec(memory_space=pl.ANY),
         ],
         out_specs=pl.BlockSpec(memory_space=pltpu.VMEM),
         scratch_shapes=[
+            pltpu.SMEM((128, 128), jnp.int32),
             pltpu.VMEM((16, 16, 256, 128), bf),
             pltpu.VMEM((16, 512, 256), bf),
             pltpu.VMEM((8, 512, 256), bf),
@@ -422,7 +488,7 @@
             pltpu.VMEM((16, 512, 256), bf),
             pltpu.VMEM((ITEMS, 512, 256), bf),
             pltpu.VMEM((ITEMS, 512, 256), bf),
-            dma((4,)),
+            dma((5,)),
             dma((CHUNKS + 1, KINDS)),
             dma((CHUNKS + 1, KINDS)),
             dma((8,)),

time: 162 us -> 152 us (0.938)
  the two profiles are of different devices: /device:TPU:81 before, /device:TPU:109 now
where the time goes in v3:
time: 152 us; the launch traced here: 151 us
  Pallas kernels  148 us (97%)
  local copies, waits for them, and re-layouts  3.08 us (2%)
    pallas_call x1, Pallas kernels, local(): pl.pallas_call(kernel, out_shape=jax.ShapeDtypeStruct((1024, 512), jnp.fl...  148 us
    unnamed x1, local copies, waits for them, and re-layouts  3.08 us

profile of v3, /device:TPU:109, one launch (start us, length us, event | category | flops | bytes accessed | tf_op | source)
XLA Modules:
  0.0 151.5 jit_solution(10387590042755746076)
XLA Ops:
  0.0 148.4 %shard_map.37 = f32[1024,512]{1,0:T(8,128)} custom-call(bf16[512,256]{1,0:T(8,128)(2,1)} %bitcast.1, bf16[16,256,128]{2,1,0:T(8,128)(2,1)} %w_ref.1, s32[128,128]{1,0:T(8,128)} %q_hbm.1), custom_call_target="tpu_custom_call" | custom-call | flops 10000000000 | bytes 4194304 | tf_op jit(solution)/shard_map/pallas_call | solution.py:473
  148.4 3.1 %copy.5 = f32[1024,512]{1,0:T(8,128)} copy(f32[1024,512]{1,0:T(8,128)} %shard_map.37) | data formatting | bytes 4194304

commit v4 on v3

--- a/solution.py
+++ b/solution.py
@@ -10,7 +10,7 @@
 MESH = pl.DeviceIdType.MESH
 NT = (((1,), (1,)), ((), ()))
 CHUNKS = 4
-AHEAD = 2
+AHEAD = 3
 KINDS = 17
 AX, AZ, BZ, BX, BS, ITEMS = 0, 12, 16, 24, 30, 32
 
@@ -197,14 +197,6 @@
     for s in range(AHEAD):
         own(s)
 
-    @pl.when(odd)
-    def _():
-        swap_d.wait()
-
-    @pl.when(jnp.logical_not(odd))
-    def _():
-        keep_d.wait()
-
     col_copies = []
 
     def col_send(i, src, who, to):
@@ -216,17 +208,33 @@
         src = dcol.at[who]
         remote(src, src, d_send.at[i], d_recv.at[i], sib).wait_recv()
 
-    col_send(0, dtmp, r, partner)
-    for i in range(1, 4):
-        col_send(i, dtmp, r, (along(i), c))
     col_own = pltpu.make_async_copy(dtmp, dcol.at[r], loc_sem.at[3])
-    col_own.start()
-
-    col_arrived(0, partner[0])
-    for i in range(1, 4):
-        col_send(3 + i, dcol.at[partner[0]], partner[0], (along(i), c))
+
+    def col_out():
+        @pl.when(odd)
+        def _():
+            swap_d.wait()
+
+        @pl.when(jnp.logical_not(odd))
+        def _():
+            keep_d.wait()
+
+        col_send(0, dtmp, r, partner)
+        for i in range(1, 4):
+            col_send(i, dtmp, r, (along(i), c))
+        col_own.start()
+
+    def col_on():
+        col_arrived(0, partner[0])
+        for i in range(1, 4):
+            col_send(3 + i, dcol.at[partner[0]], partner[0], (along(i), c))
+
     for s in range(CHUNKS):
         relay_near(s)
+        if s == 0:
+            col_out()
+        if s == 1:
+            col_on()
         if s + AHEAD < CHUNKS:
             own(s + AHEAD)
         elif s + AHEAD == CHUNKS:
@@ -472,7 +480,7 @@
     dma = pltpu.SemaphoreType.DMA
     return pl.pallas_call(
         kernel,
-        out_shape=jax.ShapeDtypeStruct((1024, 512), jnp.float32),
+        out_shape=pltpu.VMEM((1024, 512), jnp.float32),
         in_specs=[
             pl.BlockSpec(memory_space=pl.ANY),
             pl.BlockSpec(memory_space=pl.ANY),
@@ -497,7 +505,7 @@
             dma((ITEMS,)),
         ],
         compiler_params=pltpu.CompilerParams(
-            collective_id=0, has_side_effects=True, vmem_limit_bytes=60 * 2**20
+            collective_id=0, has_side_effects=True, vmem_limit_bytes=61 * 2**20
         ),
         cost_estimate=pl.CostEstimate(flops=10 * 10**9, bytes_accessed=4 * 2**20, transcendentals=0),
     )(d, screened, q_table)

time: 152 us -> 141 us (0.928)
  the two profiles are of different devices: /device:TPU:109 before, /device:TPU:81 now
where the time goes in v4:
time: 141 us; the launch traced here: 138 us
  Pallas kernels  137 us (97%)
    pallas_call x1, Pallas kernels, local(): pl.pallas_call(kernel, out_shape=pltpu.VMEM((1024, 512), jnp.float32), in...  137 us

profile of v4, /device:TPU:81, one launch (start us, length us, event | category | flops | bytes accessed | tf_op | source)
XLA Modules:
  0.0 138.3 jit_solution(3091510100862417580)
XLA Ops:
  0.0 137.0 %shard_map.37 = f32[1024,512]{1,0:T(8,128)S(1)} custom-call(bf16[512,256]{1,0:T(8,128)(2,1)} %bitcast.1, bf16[16,256,128]{2,1,0:T(8,128)(2,1)} %w_ref.1, s32[128,128]{1,0:T(8,128)} %q_hbm.1), custom_call_target="tpu_custom_call" | custom-call | flops 10000000000 | bytes 4194304 | tf_op jit(solution)/shard_map/pallas_call | solution.py:481
  137.0 1.3 copy.5

commit v5 on v4

--- a/solution.py
+++ b/solution.py
@@ -9,19 +9,19 @@
 
 MESH = pl.DeviceIdType.MESH
 NT = (((1,), (1,)), ((), ()))
-CHUNKS = 4
+SIZES = (4, 4, 4, 4)
+STARTS = (0, 4, 8, 12)
+CHUNKS = len(SIZES)
 AHEAD = 3
 KINDS = 17
 AX, AZ, BZ, BX, BS, ITEMS = 0, 12, 16, 24, 30, 32
 
 
-def kernel(d_ref, w_ref, q_hbm, out_ref, q_ref, wb, drow, dcol, dtmp, yb, pout, pin,
+def kernel(d_ref, w_ref, q_hbm, out_ref, q_ref, wb, drow, dcol, dtmp, yb, pout, pin, acc,
            loc_sem, a_send, a_recv, d_send, d_recv, p_send, p_recv):
     r, c = lax.axis_index("kr"), lax.axis_index("kc")
     x, zl = r // 2, r % 2
     zh, y, core = c // 8, (c // 2) % 4, c % 2
-    q_count = w_ref.shape[0]
-    per = q_count // CHUNKS
     odd = core == 1
     vc = jnp.where(odd, 16 - c, c)
     swap_c = jnp.where(odd, 16 - c, c)
@@ -85,8 +85,8 @@
     def part(s, who, half=None):
         if s < CHUNKS:
             if half is None:
-                return wb.at[who, pl.ds(s * per, per)]
-            return wb.at[who, pl.ds(s * per + half * (per // 2), per // 2)]
+                return wb.at[who, pl.ds(STARTS[s], SIZES[s])]
+            return wb.at[who, pl.ds(STARTS[s] + half * (SIZES[s] // 2), SIZES[s] // 2)]
         if half is None:
             return drow.at[who]
         rows = drow.shape[1] // 2
@@ -135,15 +135,18 @@
         send(s, 11, c_y2, across, 7)
         send(s, 12, c_y2, sib, 12)
 
-    def finish(s):
+    def finish(s, between=None):
         arrived(s, 5, c_zym)
         send(s, 13, c_zym, sib, 13)
         arrived(s, 6, c_zyp)
         send(s, 14, c_zyp, sib, 14)
+        if between is not None:
+            between()
         arrived(s, 7, c_zy2)
         send(s, 15, c_zy2, sib, 15)
         for i, who in enumerate(blocks):
-            arrived(s, 8 + i, who - core + (1 - core))
+            if not (between is not None and i < 5):
+                arrived(s, 8 + i, who - core + (1 - core))
 
     rows_at = CHUNKS
 
@@ -186,13 +189,27 @@
 
     def screen(s):
         def one(i, carry):
-            q = s * per + i
+            q = STARTS[s] + i
             lhs = jnp.concatenate([dcol[j] for j in range(8)], axis=1)
             rhs = jnp.concatenate([wb[j, q] for j in range(16)], axis=1)
             yb[q] = lax.dot_general(lhs, rhs, NT, preferred_element_type=jnp.float32).astype(jnp.bfloat16)
             return carry
 
-        lax.fori_loop(0, per, one, 0)
+        lax.fori_loop(0, SIZES[s], one, 0)
+
+    def screen_part(s, chips, first):
+        def one(i, carry):
+            q = STARTS[s] + i
+            lhs = jnp.concatenate([dcol[j] for j in chips], axis=1)
+            rhs = jnp.concatenate([wb[2 * j + k, q] for j in chips for k in range(2)], axis=1)
+            value = lax.dot_general(lhs, rhs, NT, preferred_element_type=jnp.float32)
+            if first:
+                acc[i] = value
+            else:
+                yb[q] = (acc[i] + value).astype(jnp.bfloat16)
+            return carry
+
+        lax.fori_loop(0, SIZES[s], one, 0)
 
     for s in range(AHEAD):
         own(s)
@@ -229,38 +246,39 @@
         for i in range(1, 4):
             col_send(3 + i, dcol.at[partner[0]], partner[0], (along(i), c))
 
-    for s in range(CHUNKS):
-        relay_near(s)
-        if s == 0:
-            col_out()
-        if s == 1:
-            col_on()
-        if s + AHEAD < CHUNKS:
-            own(s + AHEAD)
-        elif s + AHEAD == CHUNKS:
-            send(rows_at, 2, c, across, 2)
-            pl.when(zh == 0)(near_out)
-        if s >= 1:
-            relay_far(s - 1)
+    relay_near(0)
+    col_out()
+    own(3)
+    relay_near(1)
+    col_on()
+    send(rows_at, 2, c, across, 2)
+    relay_far(0)
+    relay_near(2)
+    relay_far(1)
+    relay_near(3)
+    relay_far(2)
     relay_across(0)
-    relay_far(CHUNKS - 1)
-    rows_step(near_on, cross_out, True)
-    for s in range(1, CHUNKS):
-        relay_across(s)
+    relay_far(3)
+    relay_across(1)
+    relay_across(2)
+    relay_across(3)
+    rows_step(near_out, cross_out, True)
     col_own.wait()
     for i in range(1, 4):
         col_arrived(i, along(4 - i))
         col_arrived(3 + i, 2 * ((x + 4 - i) % 4) + 1 - zl)
     for s in range(CHUNKS - 1):
         finish(s)
-        if s == 0:
-            rows_step(lambda: None, cross_on, True)
         screen(s)
+    for i, who in enumerate(blocks[:5]):
+        arrived(CHUNKS - 1, 8 + i, who - core + (1 - core))
+    chips = [who // 2 for who in blocks]
+    screen_part(CHUNKS - 1, chips[:5], True)
+    finish(CHUNKS - 1, lambda: rows_step(near_on, cross_on, True))
+    load_q.wait()
+    screen_part(CHUNKS - 1, chips[5:], False)
+    rows_step(near_out, cross_out, False)
     rows_step(near_end, cross_end, True)
-    finish(CHUNKS - 1)
-    rows_step(near_out, cross_out, False)
-    load_q.wait()
-    screen(CHUNKS - 1)
 
     def product(b, k, half):
         rhs = jnp.concatenate(
@@ -279,7 +297,8 @@
         return 4 * to + i
 
     def b_row(role, i, zl_):
-        return 4 * dest[role] + 2 * zl_ + i
+        to = dest[role] if isinstance(role, int) else jnp.where(role == 0, x_far, x_pair)
+        return 4 * to + 2 * zl_ + i
 
     def item(base, i, to):
         return remote(pout.at[base + i], pin.at[base + i], p_send.at[base + i], p_recv.at[base + i], to)
@@ -404,22 +423,54 @@
 
         each(2, lambda i: 4 * x + 2 * zk + i, body)
 
+    def left(count, row, copy, when=None):
+        def one(i, carry):
+            live = row(i) <= vc
+            if when is not None:
+                live = jnp.logical_and(live, when)
+
+            @pl.when(live)
+            def _():
+                copy(i).wait_send()
+
+            return carry
+
+        lax.fori_loop(0, count, one, 0)
+
+    def gather_left():
+        for copy in sent + col_copies:
+            copy.wait_send()
+
+    def rows_left():
+        for kind in range(KINDS):
+            ref = part(rows_at, c, 0 if kind in (4, 6, 11, 16) else None)
+            remote(ref, ref, a_send.at[rows_at, kind], a_recv.at[rows_at, kind], sib).wait_send()
+
+    def first_left():
+        for role in range(3):
+            left(4, lambda i: a_row(role, i), lambda i: item(AX + 4 * role, i, to_pair))
+        for role in range(4):
+            left(2, lambda i: b_row(role, i, 1 - zk), lambda i: item(BZ + 2 * role, i, partner))
+
     low_first = jnp.where(x >= 2, 0, 1)
     a_first(low_first)
     b_across(0)
     b_across(1)
     rows_step(near_on, cross_on, False)
+    gather_left()
     rows_step(near_end, cross_end, False)
     pl.when(x < 2)(lambda: a_first(0))
     b_across(2)
     b_across(3)
+    pl.when(x >= 2)(lambda: a_first(1))
     a_mid()
-    pl.when(x >= 2)(lambda: a_first(1))
-    b_first(0)
-    b_first(1)
+    b_first(low_first)
+    b_first(1 - low_first)
     a_final(zl, True)
     a_final(1 - zl, False)
+    rows_left()
     b_mid()
+    first_left()
     b_final()
 
     for i in range(2):
@@ -443,31 +494,8 @@
             b_home(i).wait_recv()
             out_ref[rows, :256] = pin[BS + i].astype(jnp.float32)
 
-    for copy in sent + col_copies:
-        copy.wait_send()
-    for kind in range(KINDS):
-        ref = part(rows_at, c, 0 if kind in (4, 6, 11, 16) else None)
-        remote(ref, ref, a_send.at[rows_at, kind], a_recv.at[rows_at, kind], sib).wait_send()
-
-    def left(count, row, copy, when=None):
-        def one(i, carry):
-            live = row(i) <= vc
-            if when is not None:
-                live = jnp.logical_and(live, when)
-
-            @pl.when(live)
-            def _():
-                copy(i).wait_send()
-
-            return carry
-
-        lax.fori_loop(0, count, one, 0)
-
     for role in range(3):
-        left(4, lambda i: a_row(role, i), lambda i: item(AX + 4 * role, i, to_pair))
         left(2, lambda i: b_row(role, i, zk), lambda i: item(BX + 2 * role, i, to_pair))
-    for role in range(4):
-        left(2, lambda i: b_row(role, i, 1 - zk), lambda i: item(BZ + 2 * role, i, partner))
     left(2, lambda i: 4 * x + 2 * (1 - zl) + i, lambda i: a_home(zl, 1 - zl, i))
     left(2, lambda i: 4 * x + 2 * zl + i, lambda i: a_home(zl, zl, i), odd)
     left(2, lambda i: 4 * x + 2 * zk + i, b_home, odd)
@@ -496,6 +524,7 @@
             pltpu.VMEM((16, 512, 256), bf),
             pltpu.VMEM((ITEMS, 512, 256), bf),
             pltpu.VMEM((ITEMS, 512, 256), bf),
+            pltpu.VMEM((SIZES[-1], 512, 256), jnp.float32),
             dma((5,)),
             dma((CHUNKS + 1, KINDS)),
             dma((CHUNKS + 1, KINDS)),

time: 141 us -> 136 us (0.965)
  Pallas kernels: 137 us -> 132 us
    pallas_call x1, Pallas kernels: 137 us -> 132 us  [local(): pl.pallas_call(kernel, out_shape=pltpu.VMEM((1024, 512), jnp.float32), in...]
where the time goes in v5:
time: 136 us; the launch traced here: 134 us
  Pallas kernels  132 us (97%)
    pallas_call x1, Pallas kernels, local(): pl.pallas_call(kernel, out_shape=pltpu.VMEM((1024, 512), jnp.float32), in...  132 us

profile of v5, /device:TPU:81, one launch (start us, length us, event | category | flops | bytes accessed | tf_op | source)
XLA Modules:
  0.0 133.6 jit_solution(327480313156473481)
XLA Ops:
  0.0 132.2 %shard_map.37 = f32[1024,512]{1,0:T(8,128)S(1)} custom-call(bf16[512,256]{1,0:T(8,128)(2,1)} %bitcast.1, bf16[16,256,128]{2,1,0:T(8,128)(2,1)} %w_ref.1, s32[128,128]{1,0:T(8,128)} %q_hbm.1), custom_call_target="tpu_custom_call" | custom-call | flops 10000000000 | bytes 4194304 | tf_op jit(solution)/shard_map/pallas_call | solution.py:509
  132.3 1.3 copy.5

commit v6 on v5

--- a/solution.py
+++ b/solution.py
@@ -127,7 +127,6 @@
         arrived(s, 2, c_z)
         send(s, 8, c_z, up, 5)
         send(s, 9, c_z, down, 6)
-        send(s, 10, c_z, sib, 11)
 
     def relay_far(s):
         arrived(s, 3, c_y2, 0)
@@ -167,6 +166,7 @@
 
     def cross_out():
         relay_across(rows_at)
+        send(rows_at, 10, c_z, sib, 11)
 
     def cross_on():
         arrived(rows_at, 5, c_zym)
@@ -263,6 +263,8 @@
     relay_across(2)
     relay_across(3)
     rows_step(near_out, cross_out, True)
+    for s in range(CHUNKS):
+        send(s, 10, c_z, sib, 11)
     col_own.wait()
     for i in range(1, 4):
         col_arrived(i, along(4 - i))
@@ -274,10 +276,9 @@
         arrived(CHUNKS - 1, 8 + i, who - core + (1 - core))
     chips = [who // 2 for who in blocks]
     screen_part(CHUNKS - 1, chips[:5], True)
-    finish(CHUNKS - 1, lambda: rows_step(near_on, cross_on, True))
+    finish(CHUNKS - 1, lambda: (rows_step(near_on, cross_on, True), rows_step(near_out, cross_out, False)))
     load_q.wait()
     screen_part(CHUNKS - 1, chips[5:], False)
-    rows_step(near_out, cross_out, False)
     rows_step(near_end, cross_end, True)
 
     def product(b, k, half):
@@ -453,9 +454,18 @@
             left(2, lambda i: b_row(role, i, 1 - zk), lambda i: item(BZ + 2 * role, i, partner))
 
     low_first = jnp.where(x >= 2, 0, 1)
-    a_first(low_first)
-    b_across(0)
-    b_across(1)
+    def even_order_0():
+        b_across(0)
+        b_across(1)
+        a_first(low_first)
+
+    def odd_order_0():
+        a_first(low_first)
+        b_across(0)
+        b_across(1)
+
+    pl.when(even)(even_order_0)
+    pl.when(odd)(odd_order_0)
     rows_step(near_on, cross_on, False)
     gather_left()
     rows_step(near_end, cross_end, False)

time: 136 us -> 135 us (level)
  no operation moved by 1% of the time
where the time goes in v6:
time: 135 us; the launch traced here: 134 us
  Pallas kernels  132 us (98%)
    pallas_call x1, Pallas kernels, local(): pl.pallas_call(kernel, out_shape=pltpu.VMEM((1024, 512), jnp.float32), in...  132 us

profile of v6, /device:TPU:81, one launch (start us, length us, event | category | flops | bytes accessed | tf_op | source)
XLA Modules:
  0.0 133.6 jit_solution(7840470851084226325)
XLA Ops:
  0.0 132.2 %shard_map.37 = f32[1024,512]{1,0:T(8,128)S(1)} custom-call(bf16[512,256]{1,0:T(8,128)(2,1)} %bitcast.1, bf16[16,256,128]{2,1,0:T(8,128)(2,1)} %w_ref.1, s32[128,128]{1,0:T(8,128)} %q_hbm.1), custom_call_target="tpu_custom_call" | custom-call | flops 10000000000 | bytes 4194304 | tf_op jit(solution)/shard_map/pallas_call | solution.py:519
  132.3 1.3 copy.5

commit v7 on v5

--- a/solution.py
+++ b/solution.py
@@ -491,8 +491,12 @@
             a_home(0, zl, i).wait_recv()
             a_home(1, zl, i).wait_recv()
             out_ref[rows, 256:] = pin[AZ + i].astype(jnp.float32) + pin[AZ + 2 + i].astype(jnp.float32)
+
+    for i in range(2):
+        @pl.when(jnp.logical_and(odd, 2 * r + i <= c))
+        def _():
             b_home(i).wait_recv()
-            out_ref[rows, :256] = pin[BS + i].astype(jnp.float32)
+            out_ref[pl.ds(i * 512, 512), :256] = pin[BS + i].astype(jnp.float32)
 
     for role in range(3):
         left(2, lambda i: b_row(role, i, zk), lambda i: item(BX + 2 * role, i, to_pair))

time: 136 us -> 136 us (level)
  no operation moved by 1% of the time
where the time goes in v7:
time: 136 us; the launch traced here: 134 us
  Pallas kernels  132 us (97%)
    pallas_call x1, Pallas kernels, local(): pl.pallas_call(kernel, out_shape=pltpu.VMEM((1024, 512), jnp.float32), in...  132 us

profile of v7, /device:TPU:81, one launch (start us, length us, event | category | flops | bytes accessed | tf_op | source)
XLA Modules:
  0.0 133.6 jit_solution(4576944464275572379)
XLA Ops:
  0.0 132.2 %shard_map.37 = f32[1024,512]{1,0:T(8,128)S(1)} custom-call(bf16[512,256]{1,0:T(8,128)(2,1)} %bitcast.1, bf16[16,256,128]{2,1,0:T(8,128)(2,1)} %w_ref.1, s32[128,128]{1,0:T(8,128)} %q_hbm.1), custom_call_target="tpu_custom_call" | custom-call | flops 10000000000 | bytes 4194304 | tf_op jit(solution)/shard_map/pallas_call | solution.py:513
  132.3 1.3 copy.5
